TPU v7x, 128 devices: a whole 4x4x4 slice. The times are simulated.
128 devices in a mesh: lat: 32 (over z, x, core), lon: 4 (over y).
Axes of the slice: x: 4, y: 4, z: 4, core: 2. Of those that a mesh axis runs over, the one named last changes fastest.
Arguments:
- state: float32 [512, 1440, 256], P('lat', 'lon'), may hold values from -6 to 6
- winds: bfloat16 [512, 1440, 128], P('lat', 'lon'), may hold values from -0.44921875 to 0.44921875
- decay: float32 [4], replicated, may hold values from 0.005 to 0.5
- widths: int32 [512], replicated, may hold values from 0 to 480, as said below
Outputs:
- advected: bfloat16 [512, 1440, 256], P('lat', 'lon')
Inputs may be any that keep to these rules, and one draw needn't show every extreme that they name: widths is 0 on rows 128 to 383 and at least 1 on the other rows; the first and last rows have exactly 480.
All inputs are finite; a program needn't handle non-finite values.
Results may differ from a plain program's by a relative error of at most 0.0075.
Values may be sent and summed in bfloat16 or wider, within the bound.
A program may use at most 128 MiB of HBM per device.

v0:
```python
import functools

import jax
import jax.numpy as jnp
from jax import lax
from jax.experimental import pallas as pl
from jax.experimental.pallas import tpu as pltpu
from jax.sharding import PartitionSpec as P

STEPS = 4
HALO = 2 * STEPS
MESH = pl.DeviceIdType.MESH
F32 = jnp.float32
BF16 = jnp.bfloat16
FAR = 1.0e6
FIELD_ROWS = 6
WEIGHT_ROWS = 7
TURN = (2, 1, 3, 0)


def chunks(count, size):
    return [(a, min(size, count - a)) for a in range(0, count, size)]


def band_kernel(
    dims, state, winds, decay, widths, out,
    stf, low, circ, relay, gaps, table, mat, xs, yc, ot, ext, wext, wv, wide,
    wedge, wland, eedge, eland, f0, f1, f2, f3, weights, nat, ost,
    ld, fs, fr, rl, rls, rs, rr, hs, hr, wsem, esem, wrow, osem,
):
    bands, rows, cols, pad, levels, seg = dims
    half = 2 * levels
    lat = lax.axis_index("lat")
    lon = lax.axis_index("lon")
    quarter = bands // 4
    polar = (lat < quarter) | (lat >= bands - quarter)
    inner = jnp.logical_not(polar)
    twin = jnp.where((lat // quarter) % 2 == 0, lat + quarter, lat - quarter)
    home = jnp.where(polar, lat, twin)
    odd = lat % 2
    home_odd = home % 2
    first = lat - 1 + 2 * odd
    last = lat + 1 - 2 * odd
    has_first = (first >= 0) & (first < bands)

    def at(la, lo):
        return {"lat": la, "lon": lo}

    def actual(p, flip):
        return jnp.where(flip == 1, rows - 1 - p, p)

    def remote(src, dst, send, recv, la, lo):
        return pltpu.make_async_remote_copy(
            src_ref=src, dst_ref=dst, send_sem=send, recv_sem=recv, device_id=at(la, lo), device_id_type=MESH
        )

    barrier = pltpu.get_barrier_semaphore()
    for k in range(4):
        pl.semaphore_signal(barrier, inc=1, device_id=at(twin, (lon + k) % 4), device_id_type=MESH)
        if k:
            pl.semaphore_signal(barrier, inc=1, device_id=at(lat, (lon + k) % 4), device_id_type=MESH)
    for side in (1, bands - 1):
        pl.semaphore_signal(barrier, inc=1, device_id=at((lat + side) % bands, lon), device_id_type=MESH)

    def nth_row(n):
        q, place = n // 4, n % 4
        k = jnp.where(place == 0, 2, jnp.where(place == 1, 1, jnp.where(place == 2, 3, 0)))
        return actual(4 * q + (lon + k) % 4, odd)

    def load(n):
        return pltpu.make_async_copy(state.at[nth_row(n)], stf.at[n % 4], ld.at[n % 4])

    for n in range(4):
        load(n).start()
    wind_load = pltpu.make_async_copy(winds, wv, wsem.at[0])
    wind_load.start()

    pl.semaphore_wait(barrier, 9)

    def convert(n, c):
        load(n).wait()
        i = nth_row(n)
        for h in range(2):
            lanes = slice(h * half, (h + 1) * half)
            low[i, h] = stf[n % 4, :, lanes].astype(BF16)
            eedge[0, i, h] = stf[n % 4, 0:16, lanes].astype(BF16)
            eedge[1, i, h] = stf[n % 4, cols - 16 : cols, lanes].astype(BF16)

        @pl.when(n + 4 < rows)
        def _():
            load(n + 4).start()

        return c

    def own_slot(n):
        return n - 3 if n >= 6 else (n - 1) // 2

    def shared(n):
        return n in (0, 2, 4)

    def forward(n, k):
        q, h = n // 2, n % 2
        target = (lon + k) % 4
        src = low.at[actual(4 * q + target, odd), h]
        if shared(n):
            return remote(src, relay.at[n // 2, target], fs.at[n, k], rl.at[n // 2, target], twin, lon)
        if k == 0:
            return pltpu.make_async_copy(src, circ.at[own_slot(n), lon], fr.at[own_slot(n), lon])
        return remote(src, circ.at[own_slot(n), lon], fs.at[n, k], fr.at[own_slot(n), lon], lat, target)

    def send_group(q):
        lax.fori_loop(4 * q, 4 * q + 4, convert, 0)

        @pl.when(polar)
        def _():
            for n in (2 * q, 2 * q + 1):
                for k in TURN:
                    forward(n, k).start()

    send_group(0)
    send_group(1)

    wind_load.wait()
    wedge[0] = wv[:, 0:16, :]
    wedge[1] = wv[:, cols - 16 : cols, :]

    def beside(n):
        return (lon + (3 if n == 0 else 1)) % 4

    def wind_edge(n):
        return remote(wedge.at[n], wland.at[n], wsem.at[1 + n], wsem.at[3 + n], lat, beside(n))

    def state_edge(n):
        return remote(eedge.at[n], eland.at[n], esem.at[n], esem.at[2 + n], lat, beside(n))

    for n in range(2):
        wind_edge(n).start()

    send_group(2)
    send_group(3)

    @pl.when(inner)
    def _():
        for n in range(2):
            state_edge(n).start()

    @pl.when(jnp.logical_not(has_first))
    def _():
        ext[0:HALO] = jnp.zeros((HALO, 2, seg, 8, half), BF16)
        wext[0:HALO] = jnp.zeros((HALO, seg, 8, half), BF16)

    def wind_row(i, c):
        wide[0, 0:8] = wland[1, i, 8:16, :].astype(F32)
        wide[0, pl.ds(8, cols)] = wv[i].astype(F32)
        wide[0, pl.ds(8 + cols, 16)] = wland[0, i].astype(F32)
        e = HALO + actual(i, odd)
        for j in range(seg):
            wext[e, j] = wide[0, pl.ds(j, 8, stride=seg)].astype(BF16)
        return c

    for n in range(2):
        wind_edge(n).wait()
    lax.fori_loop(0, rows, wind_row, 0)

    def wind_first(p):
        return remote(wext.at[HALO + p], wext.at[7 - p], wrow.at[0], wrow.at[1], first, lon)

    def wind_last(p):
        return remote(wext.at[HALO + p], wext.at[39 - p], wrow.at[2], wrow.at[3], last, lon)

    def all_wind_first():
        return remote(wext.at[pl.ds(8, 8)], wext.at[pl.ds(0, 8)], wrow.at[0], wrow.at[1], first, lon)

    def all_wind_last():
        return remote(wext.at[pl.ds(16, 8)], wext.at[pl.ds(24, 8)], wrow.at[2], wrow.at[3], last, lon)

    @pl.when(has_first)
    def _():
        for p in range(8):
            wind_first(p).start()

    for p in range(8, 16):
        wind_last(p).start()

    def to_first(p):
        return remote(ext.at[HALO + p], ext.at[7 - p], hs.at[p], hr.at[7 - p], first, lon)

    def to_last(p):
        return remote(ext.at[HALO + p], ext.at[39 - p], hs.at[p], hr.at[23 - p], last, lon)

    @pl.when(inner)
    def _():
        for n in range(2):
            state_edge(n).wait()

        def state_row(i, c):
            e = HALO + actual(i, odd)
            for h in range(2):
                wide[h, 0:8] = eland[1, i, h, 8:16, :].astype(F32)
                wide[h, pl.ds(8, cols)] = low[i, h].astype(F32)
                wide[h, pl.ds(8 + cols, 16)] = eland[0, i, h].astype(F32)
                for j in range(seg):
                    ext[e, h, j] = wide[h, pl.ds(j, 8, stride=seg)].astype(BF16)
            return c

        lax.fori_loop(0, rows, state_row, 0)

        def give(p, c):
            to_first(p).start()
            to_last(p + 8).start()
            return c

        lax.fori_loop(0, 8, give, 0)

    there = lax.broadcasted_iota(jnp.int32, (cols, pad), 0)
    here_ = lax.broadcasted_iota(jnp.int32, (cols, pad), 1)
    for d in range(4):
        apart = jnp.abs(there - here_ - d * cols)
        apart = jnp.minimum(apart, 4 * cols - apart).astype(F32)
        gaps[d] = jnp.where(here_ < cols, apart, FAR)

    def tabulate(n, c):
        f, d = n // 4, n % 4
        table[f, d] = jnp.exp(-decay[f] * gaps[d]).astype(BF16)
        return c

    lax.fori_loop(0, 16, tabulate, 0)
    for d in range(4):
        xs[d, pl.ds(pad - 32, 32)] = jnp.zeros((32, 4 * levels), BF16)

    def relay_copy(m, k):
        target = (lon + k) % 4
        if k == 0:
            return pltpu.make_async_copy(relay.at[m, target], circ.at[m, lon], fr.at[m, lon])
        return remote(relay.at[m, target], circ.at[m, lon], rls.at[m, k], fr.at[m, lon], lat, target)

    def pass_relay(m):
        for k in TURN:
            target = (lon + k) % 4
            pltpu.make_async_copy(low.at[0, 0], relay.at[m, target], rl.at[m, target]).wait()
            relay_copy(m, k).start()

    def placed(n):
        slot = jnp.where(n >= 6, n - 3, (n - 1) // 2)
        return slot, n // 2, jnp.where(polar, n % 2, 0)

    def returned(n, k):
        slot, q, h = placed(n)
        p = 4 * q + lon
        return remote(
            ot.at[slot, (lon + k) % 4], ext.at[HALO + p, h], rs.at[slot, k], rr.at[p, h], home, (lon + k) % 4
        )

    def filter_unit(n):
        slot, q, h = placed(n)
        i = actual(4 * q + lon, home_odd)
        reach = widths[home * rows + i].astype(F32)
        for t in range(4):
            pltpu.make_async_copy(low.at[0, 0], circ.at[slot, t], fr.at[slot, t]).wait()
        for ff in range(2):
            f = 2 * h + ff
            rate = decay[f]
            total = jnp.zeros((1, 1), F32)
            for d in range(4):
                gap = gaps[d, 0:1]
                kept = jnp.where(gap <= reach, jnp.exp(-rate * gap), 0.0)
                total = total + jnp.sum(kept, axis=1, keepdims=True)
            scale = 1.0 / total
            for d in range(4):
                mat[d] = jnp.where(gaps[d] <= reach, table[f, d].astype(F32), 0.0).astype(BF16)
                xs[d, pl.ds(0, cols)] = jnp.concatenate(
                    [circ[slot, (t + d) % 4, :, ff * levels : (ff + 1) * levels] for t in range(4)], axis=1
                )
            result = jnp.dot(mat[0], xs[0], preferred_element_type=F32)
            for d in range(1, 4):
                result = result + jnp.dot(mat[d], xs[d], preferred_element_type=F32)
            result = result * scale
            for t in range(4):
                yc[pl.ds(8 + t * cols, cols), ff * levels : (ff + 1) * levels] = result[:, t * levels : (t + 1) * levels]
        yc[0:8] = yc[pl.ds(4 * cols, 8)]
        yc[pl.ds(8 + 4 * cols, 16)] = yc[8:24]
        for t in range(4):
            for j in range(seg):
                ot[slot, t, j] = yc[pl.ds(t * cols + j, 8, stride=seg)].astype(BF16)
        for k in (2, 1, 3):
            returned(n, k).start()

        @pl.when(polar)
        def _():
            pltpu.make_async_copy(ot.at[slot, lon], ext.at[HALO + 4 * q + lon, h], rr.at[4 * q + lon, h]).start()

        @pl.when(inner)
        def _():
            returned(n, 0).start()

    def pass_on(q):
        def each(p, c):
            for h in range(2):
                pltpu.make_async_copy(ot.at[0, 0], ext.at[HALO + p, h], rr.at[p, h]).wait()

            @pl.when((p < 8) & has_first)
            def _():
                to_first(p).start()

            @pl.when(p >= 8)
            def _():
                to_last(p).start()

            return c

        lax.fori_loop(4 * q, 4 * q + 4, each, 0)

    fields = (f0, f1, f2, f3)
    upward = 1.0 - 2.0 * odd.astype(F32)

    def halo_cells(field, slot, h):
        for n in range(2):
            field[slot, h, n] = pltpu.roll(field[slot, h, seg + n], 1, 0)
            field[slot, h, seg + 2 + n] = pltpu.roll(field[slot, h, 2 + n], 7, 0)

    def written(p):
        return pltpu.make_async_copy(ost.at[p % 4], out.at[actual(p, odd)], osem.at[p % 4])

    def advance(r, c):
        slot = lax.rem(r, FIELD_ROWS)
        for h in range(2):
            for a, n in chunks(seg, 8):
                f0[slot, h, pl.ds(2 + a, n)] = ext[r, h, pl.ds(a, n)].astype(F32)
            halo_cells(f0, slot, h)

        @pl.when(r >= 4)
        def _():
            made = lax.rem(r - 2, WEIGHT_ROWS)
            for a, n in chunks(seg, 8):
                both = wext[r - 2, pl.ds(a, n)].astype(F32)
                lane = lax.broadcasted_iota(jnp.int32, (n, 8, half), 2)
                other = pltpu.roll(both, levels, 2)
                cu = jnp.where(lane < levels, both, other)
                cv = jnp.where(lane < levels, other, both)
                pairs = ((cu, cu * cu), (cv * upward, cv * cv))
                for m, (one, square) in enumerate(pairs):
                    near, near2 = (2.0 / 3.0) * one, (2.0 / 3.0) * square
                    far, far2 = (1.0 / 12.0) * one, (1.0 / 24.0) * square
                    for w, value in enumerate((near2 - near, far - far2, near2 + near, -far - far2)):
                        weights[made, 4 * m + w, pl.ds(a, n)] = value
                weights[made, 8, pl.ds(a, n)] = 1.0 - 1.25 * (pairs[0][1] + pairs[1][1])

        for s in range(1, STEPS + 1):

            @pl.when(r >= 4 * s)
            def _(s=s):
                old = fields[s - 1]
                i = r - 2 * s
                wrow_ = lax.rem(i, WEIGHT_ROWS)
                here, ahead, ahead2 = (lax.rem(i + o, FIELD_ROWS) for o in (0, 1, 2))
                behind2, behind = (lax.rem(i + o, FIELD_ROWS) for o in (4, 5))
                for a, n in chunks(seg, 4):
                    w = [weights[wrow_, m, pl.ds(a, n)] for m in range(9)]
                    for h in range(2):

                        def cell(row, shift):
                            return old[row, h, pl.ds(2 + a + shift, n)]

                        along = (w[0] * cell(here, 1) + w[1] * cell(here, 2)) + (
                            w[2] * cell(here, -1) + w[3] * cell(here, -2)
                        )
                        across = (w[4] * cell(ahead, 0) + w[5] * cell(ahead2, 0)) + (
                            w[6] * cell(behind, 0) + w[7] * cell(behind2, 0)
                        )
                        value = w[8] * cell(here, 0) + (along + across)
                        if s < STEPS:
                            fields[s][here, h, pl.ds(2 + a, n)] = value
                        else:
                            for m in range(n):
                                nat[h, pl.ds(a + m, 8, stride=seg)] = value[m]
                if s < STEPS:
                    for h in range(2):
                        halo_cells(fields[s], here, h)
                else:
                    p = r - 16

                    @pl.when(p >= 4)
                    def _():
                        written(p - 4).wait()

                    for h in range(2):
                        ost[p % 4, :, h * half : (h + 1) * half] = nat[h, pl.ds(8, cols)].astype(BF16)
                    written(p).start()

        return c

    def stage(n, c):
        for m in range(3):

            @pl.when(inner & (n == 2 * m))
            def _(m=m):
                pass_relay(m)

        @pl.when(((n % 2 == 1) & (n <= 5)) | (polar & ((n == 6) | (n == 7))))
        def _():
            filter_unit(n)

        @pl.when(polar & ((n == 3) | (n == 5) | (n == 7) | (n == 8)))
        def _():
            pass_on(jnp.where(n == 8, 3, (n - 3) // 2))

        @pl.when(n == 6)
        def _():
            all_wind_last().wait()

            @pl.when(has_first)
            def _():
                all_wind_first().wait()
                for e in range(8):
                    to_first(7 - e).wait_recv()

        @pl.when(n == 8)
        def _():
            for e in range(8, 16):
                to_last(23 - e).wait_recv()

        begin = jnp.where(n == 8, 20, jnp.where(n == 7, 6, 0))
        end = jnp.where(n == 8, 32, jnp.where(n == 7, 20, jnp.where(n == 6, 6, 0)))
        lax.fori_loop(begin, end, advance, 0)
        return c

    lax.fori_loop(0, 9, stage, 0)

    for p in range(12, 16):
        written(p).wait()

    @pl.when(polar)
    def _():
        for n in range(8):
            for k in TURN:
                if k or shared(n):
                    forward(n, k).wait_send()

    @pl.when(inner)
    def _():
        for m in range(3):
            for k in (1, 2, 3):
                relay_copy(m, k).wait_send()

    for n in (1, 3, 5, 6, 7):

        @pl.when(polar if n > 5 else n > 0)
        def _(n=n):
            for k in (1, 2, 3):
                returned(n, k).wait_send()

            @pl.when(inner)
            def _():
                returned(n, 0).wait_send()

    for p in range(8, 16):
        to_last(p).wait_send()

    @pl.when(has_first)
    def _():
        for p in range(8):
            to_first(p).wait_send()


def per_device(state, winds, decay, widths):
    rows, cols, chans = state.shape
    levels = winds.shape[2] // 2
    half = 2 * levels
    bands = lax.axis_size("lat")
    pad = cols + 24
    seg = (cols + 2 * HALO) // 8
    deep = rows + 2 * HALO
    dma = pltpu.SemaphoreType.DMA
    vm = pltpu.VMEM
    hbm = pl.BlockSpec(memory_space=pl.ANY)
    smem = pl.BlockSpec(memory_space=pltpu.SMEM)
    return pl.pallas_call(
        functools.partial(band_kernel, (bands, rows, cols, pad, levels, seg)),
        out_shape=jax.ShapeDtypeStruct((rows, cols, chans), BF16),
        in_specs=[hbm, hbm, smem, smem],
        out_specs=hbm,
        scratch_shapes=[
            vm((4, cols, chans), F32),
            vm((rows, 2, cols, half), BF16),
            vm((5, 4, cols, half), BF16),
            vm((3, 4, cols, half), BF16),
            vm((4, cols, pad), F32),
            vm((4, 4, cols, pad), BF16),
            vm((4, cols, pad), BF16),
            vm((4, pad, chans), BF16),
            vm((4 * cols + 24, half), F32),
            vm((5, 4, seg, 8, half), BF16),
            vm((deep, 2, seg, 8, half), BF16),
            vm((deep, seg, 8, half), BF16),
            vm((rows, cols, half), BF16),
            vm((2, pad, half), F32),
            vm((2, rows, 16, half), BF16),
            vm((2, rows, 16, half), BF16),
            vm((2, rows, 2, 16, half), BF16),
            vm((2, rows, 2, 16, half), BF16),
            *[vm((FIELD_ROWS, 2, seg + 4, 8, half), F32)] * STEPS,
            vm((WEIGHT_ROWS, 9, seg, 8, half), F32),
            vm((2, pad, half), F32),
            vm((4, cols, chans), BF16),
            dma((4,)), dma((8, 4)), dma((5, 4)), dma((3, 4)), dma((3, 4)), dma((5, 4)), dma((16, 2)),
            dma((16,)), dma((16,)), dma((5,)), dma((4,)), dma((4,)), dma((4,)),
        ],
        compiler_params=pltpu.CompilerParams(
            collective_id=0, has_side_effects=True, vmem_limit_bytes=60 * 2**20
        ),
        name="filter_and_advect",
    )(state, winds, decay, widths)


def solution(mesh):
    in_specs = (P("lat", "lon", None), P("lat", "lon", None), P(), P())
    out_specs = P("lat", "lon", None)
    return jax.shard_map(
        per_device, mesh=mesh, in_specs=in_specs, out_specs=out_specs, check_vma=False
    )
```

profile of v0, /device:TPU:99, one launch (start us, length us, event | category | flops | bytes accessed | tf_op | source)
XLA Modules:
  0.0 121.4 jit_solution(971800215958259812)
XLA Ops:
  0.0 117.7 %filter_and_advect.1 = bf16[16,360,256]{2,1,0:T(8,128)(2,1)} custom-call(f32[16,360,256]{2,1,0:T(8,128)} %state.1, bf16[16,360,128]{2,1,0:T(8,128)(2,1)} %winds.1, f32[4]{0:T(128)} %decay.1, s32[512]{0:T(512)} %widths.1), custom_call_target="tpu_custom_call" | custom-call | tf_op jit(solution)/shard_map/filter_and_advect/pallas_call | solution.py:477
  117.7 3.6 %copy.6 = bf16[16,360,256]{2,1,0:T(8,128)(2,1)} copy(bf16[16,360,256]{2,1,0:T(8,128)(2,1)} %filter_and_advect.1) | data formatting | bytes 5898240
where the time goes:
time: 122 us; the launch traced here: 121 us
  Pallas kernels  118 us (97%)
  local copies, waits for them, and re-layouts  3.62 us (3%)
    pallas_call x1, Pallas kernels, per_device(): pl.pallas_call(functools.partial(band_kernel, (bands, rows, cols, pad, le...  118 us
    unnamed x1, local copies, waits for them, and re-layouts  3.62 us

commit v1 on v0

--- a/solution.py
+++ b/solution.py
@@ -16,6 +16,10 @@
 FIELD_ROWS = 6
 WEIGHT_ROWS = 7
 TURN = (2, 1, 3, 0)
+SHARED = 3
+SHARED_EDGE = 1
+SWEEP = ((8, 0, 8), (9, 8, 14), (10, 14, 20), (11, 20, 32))
+LOADS = 8
 
 
 def chunks(count, size):
@@ -37,11 +41,13 @@
     inner = jnp.logical_not(polar)
     twin = jnp.where((lat // quarter) % 2 == 0, lat + quarter, lat - quarter)
     home = jnp.where(polar, lat, twin)
-    odd = lat % 2
-    home_odd = home % 2
-    first = lat - 1 + 2 * odd
-    last = lat + 1 - 2 * odd
-    has_first = (first >= 0) & (first < bands)
+    edge = (home // 2 == quarter // 2 - 1) | (home // 2 == (bands - quarter) // 2)
+    parts = jnp.where(edge, SHARED_EDGE, SHARED)
+    down = (lat + 1) % 2
+    home_down = (home + 1) % 2
+    first = lat - 1 + 2 * down
+    last = lat + 1 - 2 * down
+    has_last = (last >= 0) & (last < bands)
 
     def at(la, lo):
         return {"lat": la, "lon": lo}
@@ -65,12 +71,12 @@
     def nth_row(n):
         q, place = n // 4, n % 4
         k = jnp.where(place == 0, 2, jnp.where(place == 1, 1, jnp.where(place == 2, 3, 0)))
-        return actual(4 * q + (lon + k) % 4, odd)
+        return actual(4 * q + (lon + k) % 4, down)
 
     def load(n):
-        return pltpu.make_async_copy(state.at[nth_row(n)], stf.at[n % 4], ld.at[n % 4])
-
-    for n in range(4):
+        return pltpu.make_async_copy(state.at[nth_row(n)], stf.at[n % LOADS], ld.at[n % LOADS])
+
+    for n in range(LOADS):
         load(n).start()
     wind_load = pltpu.make_async_copy(winds, wv, wsem.at[0])
     wind_load.start()
@@ -82,43 +88,56 @@
         i = nth_row(n)
         for h in range(2):
             lanes = slice(h * half, (h + 1) * half)
-            low[i, h] = stf[n % 4, :, lanes].astype(BF16)
-            eedge[0, i, h] = stf[n % 4, 0:16, lanes].astype(BF16)
-            eedge[1, i, h] = stf[n % 4, cols - 16 : cols, lanes].astype(BF16)
-
-        @pl.when(n + 4 < rows)
-        def _():
-            load(n + 4).start()
+            low[i, h] = stf[n % LOADS, :, lanes].astype(BF16)
+            eedge[0, i, h] = stf[n % LOADS, 0:16, lanes].astype(BF16)
+            eedge[1, i, h] = stf[n % LOADS, cols - 16 : cols, lanes].astype(BF16)
+
+        @pl.when(n + LOADS < rows)
+        def _():
+            load(n + LOADS).start()
 
         return c
 
     def own_slot(n):
-        return n - 3 if n >= 6 else (n - 1) // 2
+        return n - jnp.minimum(parts, (n + 1) // 2)
 
     def shared(n):
-        return n in (0, 2, 4)
+        return parts > n // 2 if n % 2 == 0 else lat < 0
 
     def forward(n, k):
         q, h = n // 2, n % 2
         target = (lon + k) % 4
-        src = low.at[actual(4 * q + target, odd), h]
-        if shared(n):
-            return remote(src, relay.at[n // 2, target], fs.at[n, k], rl.at[n // 2, target], twin, lon)
+        src = low.at[actual(4 * q + target, down), h]
+        slot = own_slot(n)
         if k == 0:
-            return pltpu.make_async_copy(src, circ.at[own_slot(n), lon], fr.at[own_slot(n), lon])
-        return remote(src, circ.at[own_slot(n), lon], fs.at[n, k], fr.at[own_slot(n), lon], lat, target)
+            own = pltpu.make_async_copy(src, circ.at[slot, lon], fr.at[slot, lon])
+        else:
+            own = remote(src, circ.at[slot, lon], fs.at[n, k], fr.at[slot, lon], lat, target)
+        if n % 2:
+            return own, None
+        return own, remote(src, relay.at[n // 2, target], fs.at[n, k], rl.at[n // 2, target], twin, lon)
 
     def send_group(q):
+        for n in (2 * q, 2 * q + 1):
+
+            @pl.when(jnp.logical_not(shared(n)))
+            def _(n=n):
+                for k in TURN:
+                    forward(n, k)[0].start()
+
+            if n % 2 == 0:
+
+                @pl.when(shared(n))
+                def _(n=n):
+                    for k in TURN:
+                        forward(n, k)[1].start()
+
+    for q in range(2):
         lax.fori_loop(4 * q, 4 * q + 4, convert, 0)
 
         @pl.when(polar)
-        def _():
-            for n in (2 * q, 2 * q + 1):
-                for k in TURN:
-                    forward(n, k).start()
-
-    send_group(0)
-    send_group(1)
+        def _(q=q):
+            send_group(q)
 
     wind_load.wait()
     wedge[0] = wv[:, 0:16, :]
@@ -136,32 +155,47 @@
     for n in range(2):
         wind_edge(n).start()
 
-    send_group(2)
-    send_group(3)
+    lax.fori_loop(8, 16, convert, 0)
 
     @pl.when(inner)
     def _():
         for n in range(2):
             state_edge(n).start()
 
-    @pl.when(jnp.logical_not(has_first))
-    def _():
-        ext[0:HALO] = jnp.zeros((HALO, 2, seg, 8, half), BF16)
-        wext[0:HALO] = jnp.zeros((HALO, seg, 8, half), BF16)
+    there = lax.broadcasted_iota(jnp.int32, (cols, pad), 0)
+    here_ = lax.broadcasted_iota(jnp.int32, (cols, pad), 1)
+    for d in range(4):
+        apart = jnp.abs(there - here_ - d * cols)
+        apart = jnp.minimum(apart, 4 * cols - apart).astype(F32)
+        gaps[d] = jnp.where(here_ < cols, apart, FAR)
+
+    def tabulate(n, c):
+        f, d = n // 4, n % 4
+        table[f, d] = jnp.exp(-decay[f] * gaps[d]).astype(BF16)
+        return c
+
+    lax.fori_loop(0, 16, tabulate, 0)
+    for d in range(4):
+        xs[d, pl.ds(pad - 32, 32)] = jnp.zeros((32, 4 * levels), BF16)
+
+    @pl.when(polar)
+    def _():
+        send_group(2)
+
+    @pl.when(jnp.logical_not(has_last))
+    def _():
+        ext[rows + HALO : rows + 2 * HALO] = jnp.zeros((HALO, 2, seg, 8, half), BF16)
+        wext[rows + HALO : rows + 2 * HALO] = jnp.zeros((HALO, seg, 8, half), BF16)
 
     def wind_row(i, c):
         wide[0, 0:8] = wland[1, i, 8:16, :].astype(F32)
         wide[0, pl.ds(8, cols)] = wv[i].astype(F32)
         wide[0, pl.ds(8 + cols, 16)] = wland[0, i].astype(F32)
-        e = HALO + actual(i, odd)
+        e = HALO + actual(i, down)
         for j in range(seg):
             wext[e, j] = wide[0, pl.ds(j, 8, stride=seg)].astype(BF16)
         return c
 
-    for n in range(2):
-        wind_edge(n).wait()
-    lax.fori_loop(0, rows, wind_row, 0)
-
     def wind_first(p):
         return remote(wext.at[HALO + p], wext.at[7 - p], wrow.at[0], wrow.at[1], first, lon)
 
@@ -174,14 +208,6 @@
     def all_wind_last():
         return remote(wext.at[pl.ds(16, 8)], wext.at[pl.ds(24, 8)], wrow.at[2], wrow.at[3], last, lon)
 
-    @pl.when(has_first)
-    def _():
-        for p in range(8):
-            wind_first(p).start()
-
-    for p in range(8, 16):
-        wind_last(p).start()
-
     def to_first(p):
         return remote(ext.at[HALO + p], ext.at[7 - p], hs.at[p], hr.at[7 - p], first, lon)
 
@@ -194,7 +220,7 @@
             state_edge(n).wait()
 
         def state_row(i, c):
-            e = HALO + actual(i, odd)
+            e = HALO + actual(i, down)
             for h in range(2):
                 wide[h, 0:8] = eland[1, i, h, 8:16, :].astype(F32)
                 wide[h, pl.ds(8, cols)] = low[i, h].astype(F32)
@@ -207,26 +233,22 @@
 
         def give(p, c):
             to_first(p).start()
-            to_last(p + 8).start()
             return c
 
         lax.fori_loop(0, 8, give, 0)
 
-    there = lax.broadcasted_iota(jnp.int32, (cols, pad), 0)
-    here_ = lax.broadcasted_iota(jnp.int32, (cols, pad), 1)
-    for d in range(4):
-        apart = jnp.abs(there - here_ - d * cols)
-        apart = jnp.minimum(apart, 4 * cols - apart).astype(F32)
-        gaps[d] = jnp.where(here_ < cols, apart, FAR)
-
-    def tabulate(n, c):
-        f, d = n // 4, n % 4
-        table[f, d] = jnp.exp(-decay[f] * gaps[d]).astype(BF16)
-        return c
-
-    lax.fori_loop(0, 16, tabulate, 0)
-    for d in range(4):
-        xs[d, pl.ds(pad - 32, 32)] = jnp.zeros((32, 4 * levels), BF16)
+    def spread_winds():
+        for n in range(2):
+            wind_edge(n).wait()
+        lax.fori_loop(0, rows, wind_row, 0)
+
+        for p in range(8):
+            wind_first(p).start()
+
+        @pl.when(has_last)
+        def _():
+            for p in range(8, 16):
+                wind_last(p).start()
 
     def relay_copy(m, k):
         target = (lon + k) % 4
@@ -241,7 +263,7 @@
             relay_copy(m, k).start()
 
     def placed(n):
-        slot = jnp.where(n >= 6, n - 3, (n - 1) // 2)
+        slot = jnp.where(polar, n - jnp.minimum(parts, (n + 1) // 2), (n - 1) // 2)
         return slot, n // 2, jnp.where(polar, n % 2, 0)
 
     def returned(n, k):
@@ -253,7 +275,7 @@
 
     def filter_unit(n):
         slot, q, h = placed(n)
-        i = actual(4 * q + lon, home_odd)
+        i = actual(4 * q + lon, home_down)
         reach = widths[home * rows + i].astype(F32)
         for t in range(4):
             pltpu.make_async_copy(low.at[0, 0], circ.at[slot, t], fr.at[slot, t]).wait()
@@ -298,11 +320,11 @@
             for h in range(2):
                 pltpu.make_async_copy(ot.at[0, 0], ext.at[HALO + p, h], rr.at[p, h]).wait()
 
-            @pl.when((p < 8) & has_first)
+            @pl.when(p < 8)
             def _():
                 to_first(p).start()
 
-            @pl.when(p >= 8)
+            @pl.when((p >= 8) & has_last)
             def _():
                 to_last(p).start()
 
@@ -311,7 +333,7 @@
         lax.fori_loop(4 * q, 4 * q + 4, each, 0)
 
     fields = (f0, f1, f2, f3)
-    upward = 1.0 - 2.0 * odd.astype(F32)
+    upward = 1.0 - 2.0 * down.astype(F32)
 
     def halo_cells(field, slot, h):
         for n in range(2):
@@ -319,7 +341,7 @@
             field[slot, h, seg + 2 + n] = pltpu.roll(field[slot, h, 2 + n], 7, 0)
 
     def written(p):
-        return pltpu.make_async_copy(ost.at[p % 4], out.at[actual(p, odd)], osem.at[p % 4])
+        return pltpu.make_async_copy(ost.at[p % 4], out.at[actual(p, down)], osem.at[p % 4])
 
     def advance(r, c):
         slot = lax.rem(r, FIELD_ROWS)
@@ -390,41 +412,55 @@
         return c
 
     def stage(n, c):
-        for m in range(3):
-
-            @pl.when(inner & (n == 2 * m))
+        for m in range(4):
+
+            @pl.when(inner & (n == 2 * m) & (m < parts))
             def _(m=m):
                 pass_relay(m)
 
-        @pl.when(((n % 2 == 1) & (n <= 5)) | (polar & ((n == 6) | (n == 7))))
+        @pl.when(jnp.where(polar, (n < 8) & ((n % 2 == 1) | (n >= 2 * parts)), (n % 2 == 1) & (n < 2 * parts)))
         def _():
             filter_unit(n)
 
-        @pl.when(polar & ((n == 3) | (n == 5) | (n == 7) | (n == 8)))
-        def _():
-            pass_on(jnp.where(n == 8, 3, (n - 3) // 2))
-
-        @pl.when(n == 6)
+        @pl.when(polar & (n == 1))
+        def _():
+            send_group(3)
+
+        @pl.when(n == 2)
+        def _():
+            spread_winds()
+
+        @pl.when(polar & (n >= 7) & (n < 11))
+        def _():
+            pass_on(n - 7)
+
+        @pl.when(n == 8)
+        def _():
+            all_wind_first().wait()
+            for e in range(8):
+                to_first(7 - e).wait_recv()
+
+        @pl.when((n == 6) & inner)
+        def _():
+            def give(p, c):
+                to_last(p).start()
+                return c
+
+            lax.fori_loop(8, 16, give, 0)
+
+        @pl.when((n == 11) & has_last)
         def _():
             all_wind_last().wait()
-
-            @pl.when(has_first)
-            def _():
-                all_wind_first().wait()
-                for e in range(8):
-                    to_first(7 - e).wait_recv()
-
-        @pl.when(n == 8)
-        def _():
             for e in range(8, 16):
                 to_last(23 - e).wait_recv()
 
-        begin = jnp.where(n == 8, 20, jnp.where(n == 7, 6, 0))
-        end = jnp.where(n == 8, 32, jnp.where(n == 7, 20, jnp.where(n == 6, 6, 0)))
+        begin, end = 0, 0
+        for when, lo, hi in SWEEP:
+            begin, end = jnp.where(n == when, lo, begin), jnp.where(n == when, hi, end)
         lax.fori_loop(begin, end, advance, 0)
         return c
 
-    lax.fori_loop(0, 9, stage, 0)
+    lax.fori_loop(0, 12, stage, 0)
 
     for p in range(12, 16):
         written(p).wait()
@@ -432,34 +468,38 @@
     @pl.when(polar)
     def _():
         for n in range(8):
-            for k in TURN:
-                if k or shared(n):
-                    forward(n, k).wait_send()
+
+            @pl.when(jnp.logical_not(shared(n)))
+            def _(n=n):
+                for k in (1, 2, 3):
+                    forward(n, k)[0].wait_send()
+                    returned(n, k).wait_send()
+
+            if n % 2 == 0:
+
+                @pl.when(shared(n))
+                def _(n=n):
+                    for k in TURN:
+                        forward(n, k)[1].wait_send()
 
     @pl.when(inner)
     def _():
-        for m in range(3):
-            for k in (1, 2, 3):
-                relay_copy(m, k).wait_send()
-
-    for n in (1, 3, 5, 6, 7):
-
-        @pl.when(polar if n > 5 else n > 0)
-        def _(n=n):
-            for k in (1, 2, 3):
-                returned(n, k).wait_send()
-
-            @pl.when(inner)
-            def _():
-                returned(n, 0).wait_send()
-
-    for p in range(8, 16):
-        to_last(p).wait_send()
-
-    @pl.when(has_first)
-    def _():
-        for p in range(8):
-            to_first(p).wait_send()
+        for m in range(4):
+
+            @pl.when(m < parts)
+            def _(m=m):
+                for k in (1, 2, 3):
+                    relay_copy(m, k).wait_send()
+                for k in range(4):
+                    returned(2 * m + 1, k).wait_send()
+
+    for p in range(8):
+        to_first(p).wait_send()
+
+    @pl.when(has_last)
+    def _():
+        for p in range(8, 16):
+            to_last(p).wait_send()
 
 
 def per_device(state, winds, decay, widths):
@@ -480,16 +520,16 @@
         in_specs=[hbm, hbm, smem, smem],
         out_specs=hbm,
         scratch_shapes=[
-            vm((4, cols, chans), F32),
+            vm((LOADS, cols, chans), F32),
             vm((rows, 2, cols, half), BF16),
-            vm((5, 4, cols, half), BF16),
-            vm((3, 4, cols, half), BF16),
+            vm((8, 4, cols, half), BF16),
+            vm((4, 4, cols, half), BF16),
             vm((4, cols, pad), F32),
             vm((4, 4, cols, pad), BF16),
             vm((4, cols, pad), BF16),
             vm((4, pad, chans), BF16),
             vm((4 * cols + 24, half), F32),
-            vm((5, 4, seg, 8, half), BF16),
+            vm((8, 4, seg, 8, half), BF16),
             vm((deep, 2, seg, 8, half), BF16),
             vm((deep, seg, 8, half), BF16),
             vm((rows, cols, half), BF16),
@@ -502,7 +542,7 @@
             vm((WEIGHT_ROWS, 9, seg, 8, half), F32),
             vm((2, pad, half), F32),
             vm((4, cols, chans), BF16),
-            dma((4,)), dma((8, 4)), dma((5, 4)), dma((3, 4)), dma((3, 4)), dma((5, 4)), dma((16, 2)),
+            dma((LOADS,)), dma((8, 4)), dma((8, 4)), dma((4, 4)), dma((4, 4)), dma((8, 4)), dma((16, 2)),
             dma((16,)), dma((16,)), dma((5,)), dma((4,)), dma((4,)), dma((4,)),
         ],
         compiler_params=pltpu.CompilerParams(

time: 122 us -> 101 us (0.83)
  the two profiles are of different devices: /device:TPU:99 before, /device:TPU:13 now
where the time goes in v1:
time: 101 us
  Pallas kernels  97.3 us (96%)
  local copies, waits for them, and re-layouts  3.62 us (4%)
    pallas_call x1, Pallas kernels, per_device(): pl.pallas_call(functools.partial(band_kernel, (bands, rows, cols, pad, le...  97.3 us
    unnamed x1, local copies, waits for them, and re-layouts  3.62 us

profile of v1, /device:TPU:13, one launch (start us, length us, event | category | flops | bytes accessed | tf_op | source)
XLA Modules:
  0.0 100.9 jit_solution(2108142463745250534)
XLA Ops:
  0.0 97.3 %filter_and_advect.1 = bf16[16,360,256]{2,1,0:T(8,128)(2,1)} custom-call(f32[16,360,256]{2,1,0:T(8,128)} %state.1, bf16[16,360,128]{2,1,0:T(8,128)(2,1)} %winds.1, f32[4]{0:T(128)} %decay.1, s32[512]{0:T(512)} %widths.1), custom_call_target="tpu_custom_call" | custom-call | tf_op jit(solution)/shard_map/filter_and_advect/pallas_call | solution.py:517
  97.3 3.6 %copy.6 = bf16[16,360,256]{2,1,0:T(8,128)(2,1)} copy(bf16[16,360,256]{2,1,0:T(8,128)(2,1)} %filter_and_advect.1) | data formatting | bytes 5898240

commit v2 on v1

--- a/solution.py
+++ b/solution.py
@@ -18,7 +18,7 @@
 TURN = (2, 1, 3, 0)
 SHARED = 3
 SHARED_EDGE = 1
-SWEEP = ((8, 0, 8), (9, 8, 14), (10, 14, 20), (11, 20, 32))
+SWEEP = ((9, 0, 10), (10, 10, 16), (11, 16, 20), (12, 20, 32))
 LOADS = 8
 
 
@@ -69,7 +69,8 @@
         pl.semaphore_signal(barrier, inc=1, device_id=at((lat + side) % bands, lon), device_id_type=MESH)
 
     def nth_row(n):
-        q, place = n // 4, n % 4
+        group, place = n // 4, n % 4
+        q = jnp.where(group == 1, 2, jnp.where(group == 2, 1, group))
         k = jnp.where(place == 0, 2, jnp.where(place == 1, 1, jnp.where(place == 2, 3, 0)))
         return actual(4 * q + (lon + k) % 4, down)
 
@@ -98,46 +99,45 @@
 
         return c
 
-    def own_slot(n):
-        return n - jnp.minimum(parts, (n + 1) // 2)
-
-    def shared(n):
-        return parts > n // 2 if n % 2 == 0 else lat < 0
-
-    def forward(n, k):
-        q, h = n // 2, n % 2
+    def shared(u):
+        return parts > u - 4
+
+    def forward(u, k):
+        q, h = u // 2, u % 2
         target = (lon + k) % 4
         src = low.at[actual(4 * q + target, down), h]
-        slot = own_slot(n)
+        slot = u if u < 4 else u - parts
         if k == 0:
             own = pltpu.make_async_copy(src, circ.at[slot, lon], fr.at[slot, lon])
         else:
-            own = remote(src, circ.at[slot, lon], fs.at[n, k], fr.at[slot, lon], lat, target)
-        if n % 2:
+            own = remote(src, circ.at[slot, lon], fs.at[u, k], fr.at[slot, lon], lat, target)
+        if u < 4:
             return own, None
-        return own, remote(src, relay.at[n // 2, target], fs.at[n, k], rl.at[n // 2, target], twin, lon)
-
-    def send_group(q):
-        for n in (2 * q, 2 * q + 1):
-
-            @pl.when(jnp.logical_not(shared(n)))
-            def _(n=n):
+        return own, remote(src, relay.at[u - 4, target], fs.at[u, k], rl.at[u - 4, target], twin, lon)
+
+    def send_own(units):
+        for u in units:
+
+            @pl.when(jnp.logical_not(shared(u)) if u >= 4 else polar)
+            def _(u=u):
                 for k in TURN:
-                    forward(n, k)[0].start()
-
-            if n % 2 == 0:
-
-                @pl.when(shared(n))
-                def _(n=n):
-                    for k in TURN:
-                        forward(n, k)[1].start()
-
-    for q in range(2):
-        lax.fori_loop(4 * q, 4 * q + 4, convert, 0)
+                    forward(u, k)[0].start()
+
+    def send_shared(units):
+        for u in units:
+
+            @pl.when(shared(u))
+            def _(u=u):
+                for k in TURN:
+                    forward(u, k)[1].start()
+
+    for n, (own, other) in enumerate((((0, 1), ()), ((), (4, 5)), ((2, 3), ()), ((), (6, 7)))):
+        lax.fori_loop(4 * n, 4 * n + 4, convert, 0)
 
         @pl.when(polar)
-        def _(q=q):
-            send_group(q)
+        def _(own=own, other=other):
+            send_own(own)
+            send_shared(other)
 
     wind_load.wait()
     wedge[0] = wv[:, 0:16, :]
@@ -154,8 +154,6 @@
 
     for n in range(2):
         wind_edge(n).start()
-
-    lax.fori_loop(8, 16, convert, 0)
 
     @pl.when(inner)
     def _():
@@ -177,10 +175,6 @@
     lax.fori_loop(0, 16, tabulate, 0)
     for d in range(4):
         xs[d, pl.ds(pad - 32, 32)] = jnp.zeros((32, 4 * levels), BF16)
-
-    @pl.when(polar)
-    def _():
-        send_group(2)
 
     @pl.when(jnp.logical_not(has_last))
     def _():
@@ -262,9 +256,9 @@
             pltpu.make_async_copy(low.at[0, 0], relay.at[m, target], rl.at[m, target]).wait()
             relay_copy(m, k).start()
 
-    def placed(n):
-        slot = jnp.where(polar, n - jnp.minimum(parts, (n + 1) // 2), (n - 1) // 2)
-        return slot, n // 2, jnp.where(polar, n % 2, 0)
+    def placed(slot):
+        u = jnp.where(polar, jnp.where(slot < 4, slot, slot + parts), slot + 4)
+        return slot, u // 2, u % 2
 
     def returned(n, k):
         slot, q, h = placed(n)
@@ -418,23 +412,23 @@
             def _(m=m):
                 pass_relay(m)
 
-        @pl.when(jnp.where(polar, (n < 8) & ((n % 2 == 1) | (n >= 2 * parts)), (n % 2 == 1) & (n < 2 * parts)))
-        def _():
-            filter_unit(n)
+        @pl.when(jnp.where(polar, n < 8 - parts, (n % 2 == 1) & (n < 2 * parts)))
+        def _():
+            filter_unit(jnp.where(polar, n, n // 2))
 
         @pl.when(polar & (n == 1))
         def _():
-            send_group(3)
-
-        @pl.when(n == 2)
+            send_own((4, 5, 6, 7))
+
+        @pl.when(n == 1)
         def _():
             spread_winds()
 
-        @pl.when(polar & (n >= 7) & (n < 11))
-        def _():
-            pass_on(n - 7)
-
-        @pl.when(n == 8)
+        @pl.when(polar & (n >= 8) & (n < 12))
+        def _():
+            pass_on(n - 8)
+
+        @pl.when(n == 9)
         def _():
             all_wind_first().wait()
             for e in range(8):
@@ -448,7 +442,7 @@
 
             lax.fori_loop(8, 16, give, 0)
 
-        @pl.when((n == 11) & has_last)
+        @pl.when((n == 12) & has_last)
         def _():
             all_wind_last().wait()
             for e in range(8, 16):
@@ -460,27 +454,27 @@
         lax.fori_loop(begin, end, advance, 0)
         return c
 
-    lax.fori_loop(0, 12, stage, 0)
+    lax.fori_loop(0, 13, stage, 0)
 
     for p in range(12, 16):
         written(p).wait()
 
     @pl.when(polar)
     def _():
-        for n in range(8):
-
-            @pl.when(jnp.logical_not(shared(n)))
-            def _(n=n):
+        for u in range(8):
+
+            @pl.when(jnp.logical_not(shared(u)) if u >= 4 else polar)
+            def _(u=u):
                 for k in (1, 2, 3):
-                    forward(n, k)[0].wait_send()
-                    returned(n, k).wait_send()
-
-            if n % 2 == 0:
-
-                @pl.when(shared(n))
-                def _(n=n):
+                    forward(u, k)[0].wait_send()
+                    returned(u if u < 4 else u - parts, k).wait_send()
+
+            if u >= 4:
+
+                @pl.when(shared(u))
+                def _(u=u):
                     for k in TURN:
-                        forward(n, k)[1].wait_send()
+                        forward(u, k)[1].wait_send()
 
     @pl.when(inner)
     def _():
@@ -491,7 +485,7 @@
                 for k in (1, 2, 3):
                     relay_copy(m, k).wait_send()
                 for k in range(4):
-                    returned(2 * m + 1, k).wait_send()
+                    returned(m, k).wait_send()
 
     for p in range(8):
         to_first(p).wait_send()

time: 101 us -> 104 us (1.030)
  the two profiles are of different devices: /device:TPU:13 before, /device:TPU:32 now
where the time goes in v2:
time: 104 us
  Pallas kernels  100 us (96%)
  local copies, waits for them, and re-layouts  3.62 us (3%)
    pallas_call x1, Pallas kernels, per_device(): pl.pallas_call(functools.partial(band_kernel, (bands, rows, cols, pad, le...  100 us
    unnamed x1, local copies, waits for them, and re-layouts  3.62 us

profile of v2, /device:TPU:32, one launch (start us, length us, event | category | flops | bytes accessed | tf_op | source)
XLA Modules:
  0.0 104.0 jit_solution(16222124918094844649)
XLA Ops:
  0.0 100.4 %filter_and_advect.1 = bf16[16,360,256]{2,1,0:T(8,128)(2,1)} custom-call(f32[16,360,256]{2,1,0:T(8,128)} %state.1, bf16[16,360,128]{2,1,0:T(8,128)(2,1)} %winds.1, f32[4]{0:T(128)} %decay.1, s32[512]{0:T(512)} %widths.1), custom_call_target="tpu_custom_call" | custom-call | tf_op jit(solution)/shard_map/filter_and_advect/pallas_call | solution.py:511
  100.4 3.6 %copy.6 = bf16[16,360,256]{2,1,0:T(8,128)(2,1)} copy(bf16[16,360,256]{2,1,0:T(8,128)(2,1)} %filter_and_advect.1) | data formatting | bytes 5898240

commit v3 on v1

--- a/solution.py
+++ b/solution.py
@@ -117,8 +117,8 @@
             return own, None
         return own, remote(src, relay.at[n // 2, target], fs.at[n, k], rl.at[n // 2, target], twin, lon)
 
-    def send_group(q):
-        for n in (2 * q, 2 * q + 1):
+    def send(units):
+        for n in units:
 
             @pl.when(jnp.logical_not(shared(n)))
             def _(n=n):
@@ -132,12 +132,18 @@
                     for k in TURN:
                         forward(n, k)[1].start()
 
+    def sent(n):
+        @pl.when(shared(n))
+        def _():
+            for k in TURN:
+                forward(n, k)[1].wait_send()
+
     for q in range(2):
         lax.fori_loop(4 * q, 4 * q + 4, convert, 0)
 
         @pl.when(polar)
         def _(q=q):
-            send_group(q)
+            send((0, 1) if q == 0 else (3,))
 
     wind_load.wait()
     wedge[0] = wv[:, 0:16, :]
@@ -177,10 +183,6 @@
     lax.fori_loop(0, 16, tabulate, 0)
     for d in range(4):
         xs[d, pl.ds(pad - 32, 32)] = jnp.zeros((32, 4 * levels), BF16)
-
-    @pl.when(polar)
-    def _():
-        send_group(2)
 
     @pl.when(jnp.logical_not(has_last))
     def _():
@@ -412,6 +414,10 @@
         return c
 
     def stage(n, c):
+        @pl.when(n == jnp.where(polar, 4, 0))
+        def _():
+            spread_winds()
+
         for m in range(4):
 
             @pl.when(inner & (n == 2 * m) & (m < parts))
@@ -424,11 +430,14 @@
 
         @pl.when(polar & (n == 1))
         def _():
-            send_group(3)
-
-        @pl.when(n == 2)
-        def _():
-            spread_winds()
+            sent(0)
+            send((2,))
+
+        @pl.when(polar & (n == 3))
+        def _():
+            send((5,))
+            sent(2)
+            send((4, 6, 7))
 
         @pl.when(polar & (n >= 7) & (n < 11))
         def _():
@@ -475,12 +484,8 @@
                     forward(n, k)[0].wait_send()
                     returned(n, k).wait_send()
 
-            if n % 2 == 0:
-
-                @pl.when(shared(n))
-                def _(n=n):
-                    for k in TURN:
-                        forward(n, k)[1].wait_send()
+            if n in (4, 6):
+                sent(n)
 
     @pl.when(inner)
     def _():

time: 101 us -> 105 us (1.040)
  the two profiles are of different devices: /device:TPU:13 before, /device:TPU:32 now
where the time goes in v3:
time: 105 us
  Pallas kernels  102 us (97%)
  local copies, waits for them, and re-layouts  3.62 us (3%)
    pallas_call x1, Pallas kernels, per_device(): pl.pallas_call(functools.partial(band_kernel, (bands, rows, cols, pad, le...  102 us
    unnamed x1, local copies, waits for them, and re-layouts  3.62 us

profile of v3, /device:TPU:32, one launch (start us, length us, event | category | flops | bytes accessed | tf_op | source)
XLA Modules:
  0.0 105.2 jit_solution(13305284945256340140)
XLA Ops:
  0.0 101.5 %filter_and_advect.1 = bf16[16,360,256]{2,1,0:T(8,128)(2,1)} custom-call(f32[16,360,256]{2,1,0:T(8,128)} %state.1, bf16[16,360,128]{2,1,0:T(8,128)(2,1)} %winds.1, f32[4]{0:T(128)} %decay.1, s32[512]{0:T(512)} %widths.1), custom_call_target="tpu_custom_call" | custom-call | tf_op jit(solution)/shard_map/filter_and_advect/pallas_call | solution.py:522
  101.6 3.6 %copy.6 = bf16[16,360,256]{2,1,0:T(8,128)(2,1)} copy(bf16[16,360,256]{2,1,0:T(8,128)(2,1)} %filter_and_advect.1) | data formatting | bytes 5898240

commit v4 on v1

--- a/solution.py
+++ b/solution.py
@@ -17,7 +17,7 @@
 WEIGHT_ROWS = 7
 TURN = (2, 1, 3, 0)
 SHARED = 3
-SHARED_EDGE = 1
+SHARED_EDGE = 2
 SWEEP = ((8, 0, 8), (9, 8, 14), (10, 14, 20), (11, 20, 32))
 LOADS = 8
 
@@ -233,6 +233,7 @@
 
         def give(p, c):
             to_first(p).start()
+            to_last(p + 8).start()
             return c
 
         lax.fori_loop(0, 8, give, 0)
@@ -439,14 +440,6 @@
             all_wind_first().wait()
             for e in range(8):
                 to_first(7 - e).wait_recv()
-
-        @pl.when((n == 6) & inner)
-        def _():
-            def give(p, c):
-                to_last(p).start()
-                return c
-
-            lax.fori_loop(8, 16, give, 0)
 
         @pl.when((n == 11) & has_last)
         def _():

time: 101 us -> 106 us (1.050)
  the two profiles are of different devices: /device:TPU:13 before, /device:TPU:32 now
where the time goes in v4:
time: 106 us
  Pallas kernels  102 us (96%)
  local copies, waits for them, and re-layouts  3.62 us (3%)
    pallas_call x1, Pallas kernels, per_device(): pl.pallas_call(functools.partial(band_kernel, (bands, rows, cols, pad, le...  102 us
    unnamed x1, local copies, waits for them, and re-layouts  3.62 us

profile of v4, /device:TPU:32, one launch (start us, length us, event | category | flops | bytes accessed | tf_op | source)
XLA Modules:
  0.0 106.0 jit_solution(16484721123584254494)
XLA Ops:
  0.0 102.3 %filter_and_advect.1 = bf16[16,360,256]{2,1,0:T(8,128)(2,1)} custom-call(f32[16,360,256]{2,1,0:T(8,128)} %state.1, bf16[16,360,128]{2,1,0:T(8,128)(2,1)} %winds.1, f32[4]{0:T(128)} %decay.1, s32[512]{0:T(512)} %widths.1), custom_call_target="tpu_custom_call" | custom-call | tf_op jit(solution)/shard_map/filter_and_advect/pallas_call | solution.py:510
  102.3 3.6 %copy.6 = bf16[16,360,256]{2,1,0:T(8,128)(2,1)} copy(bf16[16,360,256]{2,1,0:T(8,128)(2,1)} %filter_and_advect.1) | data formatting | bytes 5898240

commit v5 on v4

--- a/solution.py
+++ b/solution.py
@@ -17,7 +17,7 @@
 WEIGHT_ROWS = 7
 TURN = (2, 1, 3, 0)
 SHARED = 3
-SHARED_EDGE = 2
+SHARED_EDGE = 1
 SWEEP = ((8, 0, 8), (9, 8, 14), (10, 14, 20), (11, 20, 32))
 LOADS = 8
 

time: 106 us -> 101 us (0.953)
  the two profiles are of different devices: /device:TPU:32 before, /device:TPU:13 now
where the time goes in v5:
time: 101 us
  Pallas kernels  97.3 us (96%)
  local copies, waits for them, and re-layouts  3.62 us (4%)
    pallas_call x1, Pallas kernels, per_device(): pl.pallas_call(functools.partial(band_kernel, (bands, rows, cols, pad, le...  97.3 us
    unnamed x1, local copies, waits for them, and re-layouts  3.62 us

profile of v5, /device:TPU:13, one launch (start us, length us, event | category | flops | bytes accessed | tf_op | source)
XLA Modules:
  0.0 100.9 jit_solution(15461411292100334556)
XLA Ops:
  0.0 97.3 %filter_and_advect.1 = bf16[16,360,256]{2,1,0:T(8,128)(2,1)} custom-call(f32[16,360,256]{2,1,0:T(8,128)} %state.1, bf16[16,360,128]{2,1,0:T(8,128)(2,1)} %winds.1, f32[4]{0:T(128)} %decay.1, s32[512]{0:T(512)} %widths.1), custom_call_target="tpu_custom_call" | custom-call | tf_op jit(solution)/shard_map/filter_and_advect/pallas_call | solution.py:510
  97.3 3.6 %copy.6 = bf16[16,360,256]{2,1,0:T(8,128)(2,1)} copy(bf16[16,360,256]{2,1,0:T(8,128)(2,1)} %filter_and_advect.1) | data formatting | bytes 5898240
